TPU v7x, 32 devices: a whole 2x2x4 slice. The times are simulated.
32 devices in a mesh: group: 2 (over y), depth: 8 (over z, x), tile: 2 (over core).
Axes of the slice: x: 2, y: 2, z: 4, core: 2. Of those that a mesh axis runs over, the one named last changes fastest.
Arguments:
- volume: bfloat16 [8, 6, 64, 8, 256], P('depth', None, 'group', None, 'tile'), parts along dimension 2, may hold values from -6 to 6
- dw_weight: bfloat16 [32, 7, 7, 7], replicated, may hold values from -0.3125 to 0.3125
- up_weight: bfloat16 [128, 32], replicated, may hold values from -1 to 1
- down_weight: bfloat16 [32, 128], replicated, may hold values from -0.5 to 0.5
- tap_weight: bfloat16 [3, 32, 32], replicated, may hold values from -0.625 to 0.625
- opacity_weight: float32 [32], replicated, may hold values from -1 to 1
- decode_weight: bfloat16 [32, 32, 3, 3], replicated, may hold values from -0.375 to 0.375
- out_weight: bfloat16 [3, 32], replicated, may hold values from -1 to 1
Outputs:
- rgb: float32 [6, 16, 256], P('group', 'depth', 'tile'), parts along dimension 0
There are 2 independent parts, one for each index of `group`. A program takes and returns all parts, laid end to end along the dimension named above; an argument that names none is the same for every part. Nothing has to cross between parts.
All inputs are finite; a program needn't handle non-finite values.
Results may differ from a plain program's by a relative error of at most 0.012.
Values may be sent and summed in bfloat16 or wider, within the bound.
A program may use at most 64 MiB of HBM per device.

v0:
```python
import functools

import jax
import jax.numpy as jnp
from jax import lax
from jax.experimental import pallas as pl
from jax.experimental.pallas import tpu as pltpu
from jax.sharding import PartitionSpec as P

BF = jnp.bfloat16
F32 = jnp.float32
GROUPS = 4


def iota(shape, dim):
    return lax.broadcasted_iota(jnp.int32, shape, dim)


def dot(a, b):
    return jnp.dot(a, b, preferred_element_type=F32)


def gelu(x):
    return 0.5 * x * (1.0 + jnp.tanh(0.7978845608028654 * (x + 0.044715 * (x * x * x))))


def spread_rows(weight):
    m, n = weight.shape
    left = ((iota((8 * m, m), 0) >> 3) == iota((8 * m, m), 1)).astype(F32).astype(BF)
    right = (iota((n, 8 * n), 0) == (iota((n, 8 * n), 1) >> 3)).astype(F32).astype(BF)
    full = dot(dot(left, weight).astype(BF), right)
    same = (iota(full.shape, 0) & 7) == (iota(full.shape, 1) & 7)
    return jnp.where(same, full, 0.0).astype(BF)


def shift_sum(main, halo, taps, rows):
    lane = iota((rows, 128), 1)
    total = None
    for k in range(taps):
        s = k - taps // 2
        m = main[k * rows : (k + 1) * rows]
        if s:
            h = halo[k * rows : (k + 1) * rows]
            pick = lane < s if s > 0 else lane >= 128 + s
            m = pltpu.roll(jnp.where(pick, h, m), (128 - s) % 128, 1)
        total = m if total is None else total + m
    return total


def kernel(
    bands, slabs,
    vol, taps, up, down, tap, opacity, dec, outw,
    rgb,
    front, back, upo, dno, belo, abov, base, toep, xs, xh, spread, ku, kd, kt,
    mixed, color, pieces, gathered, flat, near,
    plane_s, plane_r, row_s, row_r, col_s, col_r, mix_s, mix_r, comp_s, comp_r, img_s, img_r,
):
    planes = vol.shape[0]
    g = lax.axis_index("group")
    me = lax.axis_index("depth")
    t = lax.axis_index("tile")
    slab, band = me // bands, me % bands
    count = bands * slabs
    r = 8 // slabs
    other = 1 - t

    def at(position, tile):
        return (g, position, tile)

    has = {
        "next": slab < slabs - 1, "prev": slab > 0,
        "below": band < bands - 1, "above": band > 0,
        "after": me < count - 1, "before": me > 0,
    }
    bar = pltpu.get_barrier_semaphore()

    def greet(position, tile):
        pl.semaphore_signal(
            bar, inc=1, device_id=at(position, tile), device_id_type=pl.DeviceIdType.MESH
        )

    def both(cond, fn):
        pl.when(cond)(fn)

    greet(me, other)
    both(has["next"], lambda: greet(me + bands, t))
    both(has["prev"], lambda: greet(me - bands, t))
    both(has["below"], lambda: greet(me + 1, t))
    both(has["above"], lambda: greet(me - 1, t))
    for q in range(2):
        tile = t if q == 0 else other
        both(has["after"], lambda tile=tile: greet(me + 1, tile))
        both(has["before"], lambda tile=tile: greet(me - 1, tile))
    my_band, my_piece = me // slabs, me % slabs
    for s in range(slabs):
        src = s * bands + my_band
        both(src != me, lambda src=src: greet(src, t))
    one, two = jnp.int32(1), jnp.int32(2)
    total = one
    for name, amount in (("next", one), ("prev", one), ("below", one), ("above", one),
                         ("after", two), ("before", two)):
        total = total + jnp.where(has[name], amount, 0)
    for j in range(slabs):
        total = total + jnp.where(band * slabs + j != me, one, 0)
    pl.semaphore_wait(bar, total)

    def copy(src, dst, ss, rs, position, tile):
        return pltpu.make_async_remote_copy(
            src_ref=src, dst_ref=dst, send_sem=ss, recv_sem=rs,
            device_id=at(position, tile), device_id_type=pl.DeviceIdType.MESH,
        )

    def zero(ref):
        ref[...] = jnp.zeros(ref.shape, ref.dtype)

    to_next = copy(vol.at[planes - 3 : planes], front, plane_s.at[0], plane_r.at[0], me + bands, t)
    to_prev = copy(vol.at[0:3], back, plane_s.at[1], plane_r.at[1], me - bands, t)
    both(has["next"], to_next.start)
    both(has["prev"], to_prev.start)

    sub = iota((16, 8, 128), 1)

    def pack_rows(ref, start, n):
        def one(i, carry):
            x = ref[i].astype(F32).reshape(16, 2, 8, 128)
            a, b = x[:, 0], x[:, 1]
            low = jnp.where(sub < 4, a, pltpu.roll(b, 4, 1))
            high = jnp.where(sub < 4, pltpu.roll(a, 4, 1), b)
            upo[start + i] = low.reshape(128, 128).astype(BF)
            dno[start + i] = high.reshape(128, 128).astype(BF)
            return carry

        lax.fori_loop(0, n, one, 0)

    def row_copies(k, start, n):
        return (
            copy(upo.at[start : start + n], belo.at[start : start + n],
                 row_s.at[0, k], row_r.at[0, k], me - 1, t),
            copy(dno.at[start : start + n], abov.at[start : start + n],
                 row_s.at[1, k], row_r.at[1, k], me + 1, t),
        )

    rows = [row_copies(0, 3, planes), row_copies(1, 0, 3), row_copies(2, 3 + planes, 3)]

    def send_rows(k):
        both(has["above"], rows[k][0].start)
        both(has["below"], rows[k][1].start)

    pack_rows(vol, 3, planes)
    send_rows(0)
    both(jnp.logical_not(has["prev"]), lambda: zero(front))
    both(jnp.logical_not(has["next"]), lambda: zero(back))
    both(jnp.logical_not(has["below"]), lambda: zero(belo))
    both(jnp.logical_not(has["above"]), lambda: zero(abov))

    def build_base():
        for h in range(8):
            row, lane = iota((64, 128), 0), iota((64, 128), 1)
            dh = ((lane & 15) - h + 3) & 15
            hit = (row == (lane >> 4) * 7 + dh) & (dh < 7) & (lane < 112)
            base[h * 224 : (h + 1) * 224] = dot(taps[...], hit.astype(F32).astype(BF))

    def build_toeplitz():
        lane = iota((8, 128), 1)

        def one(c, carry):
            for k in range(7):
                b = base[pl.ds(k * 32 + c, 8, stride=224), :]
                low, high = [], []
                for p in range(planes):
                    moved = pltpu.roll(b, 16 * p, 1) if p else b
                    low.append(jnp.where(lane >= 16 * p, moved, 0.0))
                    high.append(jnp.where(lane < 16 * p, moved, 0.0))
                toep[c, k * 48 : (k + 1) * 48, 0:128] = jnp.concatenate(low, 0).astype(BF)
                toep[c, k * 48 : (k + 1) * 48, 128:256] = jnp.concatenate(high, 0).astype(BF)
            return carry

        lax.fori_loop(0, 32, one, 0)

    build_base()

    both(has["prev"], to_next.wait_recv)
    pack_rows(front, 0, 3)
    send_rows(1)
    both(has["next"], to_prev.wait_recv)
    pack_rows(back, 3 + planes, 3)
    send_rows(2)

    build_toeplitz()
    ku[...] = spread_rows(up[...])
    kd[...] = spread_rows(down[...])
    for k in range(3):
        kt[:, k * 256 : (k + 1) * 256] = spread_rows(tap[k])

    for k in range(3):
        both(has["below"], rows[k][0].wait_recv)
        both(has["above"], rows[k][1].wait_recv)

    per = 32 // GROUPS
    cols = [
        copy(xs.at[q * per : (q + 1) * per], xh.at[q * per : (q + 1) * per],
             col_s.at[q], col_r.at[q], me, other)
        for q in range(GROUPS)
    ]
    small = iota((per // 2, 8, 128), 1)
    for q in range(GROUPS):
        for p in range(planes + 6):
            ref, i = (front, p) if p < 3 else (vol, p - 3) if p < 3 + planes else (back, p - 3 - planes)
            own = ref[i, q * per * 8 : (q + 1) * per * 8].astype(F32).reshape(per // 2, 2, 8, 128)
            lo = belo[p, q * per * 4 : (q + 1) * per * 4].astype(F32).reshape(per // 2, 8, 128)
            hi = abov[p, q * per * 4 : (q + 1) * per * 4].astype(F32).reshape(per // 2, 8, 128)
            a = jnp.where(small < 4, lo, pltpu.roll(hi, 4, 1))
            b = jnp.where(small < 4, pltpu.roll(lo, 4, 1), hi)
            for j in range(per // 2):
                c = q * per + 2 * j
                xs[c, p * 16 : (p + 1) * 16] = jnp.concatenate([own[j, 0], a[j]], 0).astype(BF)
                xs[c + 1, p * 16 : (p + 1) * 16] = jnp.concatenate([own[j, 1], b[j]], 0).astype(BF)
        cols[q].start()

    depth_rows = 16 * (planes + 6)

    def outer(x, n):
        lane = iota((n, 128), 1)
        keep = (lane < 3 + 125 * t) & (lane >= 125 * t)
        return jnp.where(keep, x.astype(F32), 0.0).astype(BF)

    for q in range(GROUPS):
        cols[q].wait_recv()

        def conv(c, carry):
            cells = jnp.concatenate([xs[c], outer(xh[c], depth_rows)], 1)
            part = dot(toep[c, :, 0:128], cells[0:128]) + dot(
                toep[c, :, 128:depth_rows], cells[128:depth_rows]
            )
            total = shift_sum(part[:, 0:128], part[:, 128:256], 7, 48)
            for p in range(planes):
                spread[p, pl.ds(pl.multiple_of(c * 8, 8), 8)] = total[p * 8 : (p + 1) * 8]
            return carry

        lax.fori_loop(q * per, (q + 1) * per, conv, 0)

    def mix(p):
        s = spread[p].reshape(32, 8, 128)
        square = jnp.sum(s * s, axis=0) * (1.0 / 32)
        normed = (s * lax.rsqrt(square + 1e-05)[None]).reshape(256, 128).astype(BF)
        hidden = gelu(dot(ku[...], normed)).astype(BF)
        mixed[p + 1] = (vol[p].astype(F32) + dot(kd[...], hidden)).astype(BF)

    mix_next = copy(mixed.at[planes], mixed.at[0], mix_s.at[0], mix_r.at[0], me + bands, t)
    mix_prev = copy(mixed.at[1], mixed.at[planes + 1], mix_s.at[1], mix_r.at[1], me - bands, t)

    @pl.when(jnp.logical_not(has["prev"]))
    def _():
        mixed[0] = jnp.zeros((256, 128), BF)

    @pl.when(jnp.logical_not(has["next"]))
    def _():
        mixed[planes + 1] = jnp.zeros((256, 128), BF)

    def edge(i, carry):
        mix(i * (planes - 1))
        return carry

    lax.fori_loop(0, 2, edge, 0)
    both(has["next"], mix_next.start)
    both(has["prev"], mix_prev.start)

    def inner(p, carry):
        mix(p)
        return carry

    lax.fori_loop(1, planes - 1, inner, 0)
    both(has["prev"], mix_next.wait_recv)
    both(has["next"], mix_prev.wait_recv)

    scale = 4.0 / (planes * slabs)
    light = jnp.ones((8, 128), F32)
    color[...] = jnp.zeros((256, 128), F32)
    for p in range(planes):
        glow = dot(kt[...], mixed[p : p + 3].reshape(768, 128)).reshape(32, 8, 128)
        logit = opacity[0] * glow[0]
        for c in range(1, 32):
            logit = logit + opacity[c] * glow[c]
        alpha = scale / (1.0 + jnp.exp(-logit))
        color[...] += ((light * alpha)[None] * glow).reshape(256, 128)
        light = light * (1.0 - alpha)
    for h in range(8):
        pieces[h, 0:32] = color[pl.ds(h, 32, stride=8), :]
        pieces[h, 32:40] = jnp.broadcast_to(light[h : h + 1], (8, 128))

    sent = []
    for j in range(slabs):
        owner = band * slabs + j
        send = copy(pieces.at[j * r : (j + 1) * r], gathered.at[slab],
                    comp_s.at[j], comp_r.at[slab], owner, t)
        both(owner != me, send.start)
        sent.append((owner, send))

        @pl.when(owner == me)
        def _(j=j):
            gathered[slab] = pieces[j * r : (j + 1) * r]

    for s in range(slabs):
        src = s * bands + my_band
        take = copy(pieces.at[0:r], gathered.at[s], comp_s.at[0], comp_r.at[s], me, other)
        both(src != me, take.wait_recv)

    for y in range(r):
        image = gathered[0, y, 0:32]
        light_y = gathered[0, y, 32:33]
        for s in range(1, slabs):
            image = image + light_y * gathered[s, y, 0:32]
            light_y = light_y * gathered[s, y, 32:33]
        square = jnp.sum(image * image, axis=0, keepdims=True) * (1.0 / 32)
        flat[y] = (image * lax.rsqrt(square + 1e-05)).astype(BF)

    def img(slot, position, tile):
        return copy(flat, near.at[slot], img_s.at[slot], img_r.at[slot], position, tile)

    halo = [
        ("after", "before", img(0, me + 1, t)), ("before", "after", img(1, me - 1, t)),
        (None, None, img(2, me, other)),
        ("after", "before", img(3, me + 1, other)), ("before", "after", img(4, me - 1, other)),
    ]
    for to, _, c in halo:
        if to is None:
            c.start()
        else:
            both(has[to], c.start)
    for slot in (0, 3):
        both(jnp.logical_not(has["before"]), lambda slot=slot: zero(near.at[slot]))
    for slot in (1, 4):
        both(jnp.logical_not(has["after"]), lambda slot=slot: zero(near.at[slot]))
    for _, frm, c in halo:
        if frm is None:
            c.wait_recv()
        else:
            both(has[frm], c.wait_recv)

    lines = [jnp.concatenate([near[0, r - 1], outer(near[3, r - 1], 32)], 1)]
    for y in range(r):
        lines.append(jnp.concatenate([flat[y], outer(near[2, y], 32)], 1))
    lines.append(jnp.concatenate([near[1, 0], outer(near[4, 0], 32)], 1))
    for y in range(r):
        part = dot(dec[...], jnp.concatenate(lines[y : y + 3], 0))
        decoded = gelu(shift_sum(part[:, 0:128], part[:, 128:256], 3, 32)).astype(BF)
        values = dot(outw[...], decoded)
        for o in range(3):
            rgb[o, y : y + 1] = values[o : o + 1]

    both(has["next"], to_next.wait_send)
    both(has["prev"], to_prev.wait_send)
    for k in range(3):
        both(has["above"], rows[k][0].wait_send)
        both(has["below"], rows[k][1].wait_send)
    for q in range(GROUPS):
        cols[q].wait_send()
    both(has["next"], mix_next.wait_send)
    both(has["prev"], mix_prev.wait_send)
    for owner, send in sent:
        both(owner != me, send.wait_send)
    for to, _, c in halo:
        if to is None:
            c.wait_send()
        else:
            both(has[to], c.wait_send)


def body(
    volume, dw_weight, up_weight, down_weight, tap_weight, opacity_weight, decode_weight, out_weight
):
    planes = volume.shape[1]
    count = lax.axis_size("depth")
    bands = max(2, count // 8)
    slabs = count // bands
    r = 8 // slabs
    vol = volume.reshape(planes, 256, 128)
    taps = jnp.pad(jnp.transpose(dw_weight, (3, 0, 1, 2)).reshape(224, 49), ((0, 0), (0, 15)))
    dec = jnp.transpose(decode_weight, (3, 0, 2, 1)).reshape(96, 96)
    outw = jnp.pad(out_weight, ((0, 13), (0, 0)))
    all_planes = planes + 6
    vmem = pl.BlockSpec(memory_space=pltpu.VMEM)
    smem = pl.BlockSpec(memory_space=pltpu.SMEM)
    dma = pltpu.SemaphoreType.DMA
    return pl.pallas_call(
        functools.partial(kernel, bands, slabs),
        out_shape=jax.ShapeDtypeStruct((3, r, 128), F32),
        in_specs=[vmem, vmem, vmem, vmem, vmem, smem, vmem, vmem],
        out_specs=vmem,
        scratch_shapes=[
            pltpu.VMEM((3, 256, 128), BF), pltpu.VMEM((3, 256, 128), BF),
            pltpu.VMEM((all_planes, 128, 128), BF), pltpu.VMEM((all_planes, 128, 128), BF),
            pltpu.VMEM((all_planes, 128, 128), BF), pltpu.VMEM((all_planes, 128, 128), BF),
            pltpu.VMEM((8 * 224, 128), F32),
            pltpu.VMEM((32, 336, 256), BF),
            pltpu.VMEM((32, 16 * all_planes, 128), BF), pltpu.VMEM((32, 16 * all_planes, 128), BF),
            pltpu.VMEM((planes, 256, 128), F32),
            pltpu.VMEM((1024, 256), BF), pltpu.VMEM((256, 1024), BF), pltpu.VMEM((256, 768), BF),
            pltpu.VMEM((planes + 2, 256, 128), BF),
            pltpu.VMEM((256, 128), F32),
            pltpu.VMEM((8, 40, 128), F32), pltpu.VMEM((slabs, r, 40, 128), F32),
            pltpu.VMEM((r, 32, 128), BF), pltpu.VMEM((5, r, 32, 128), BF),
            dma((2,)), dma((2,)), dma((2, 3)), dma((2, 3)), dma((GROUPS,)), dma((GROUPS,)),
            dma((2,)), dma((2,)), dma((slabs,)), dma((slabs,)), dma((5,)), dma((5,)),
        ],
        compiler_params=pltpu.CompilerParams(
            collective_id=0, has_side_effects=True, vmem_limit_bytes=40 * 1024 * 1024
        ),
    )(vol, taps, up_weight, down_weight, tap_weight, opacity_weight, dec, outw)


def solution(mesh):
    in_specs = (P("depth", None, "group", None, "tile"), P(), P(), P(), P(), P(), P(), P())
    out_specs = P("group", "depth", "tile")
    return jax.shard_map(body, mesh=mesh, in_specs=in_specs, out_specs=out_specs, check_vma=False)
```

profile of v0, /device:TPU:0, one launch (start us, length us, event | category | flops | bytes accessed | tf_op | source)
XLA Modules:
  0.0 49.9 jit_solution(18158924729157397819)
XLA Ops:
  0.0 0.0 copy-start
  0.0 1.1 %reshape.10 = bf16[224,49]{0,1:T(8,128)(2,1)S(1)} reshape(bf16[7,32,7,7]{1,0,3,2:T(8,128)(2,1)} %bitcast.6) | data formatting | bytes 43904 | tf_op jit(solution)/shard_map/reshape | solution.py:378
  1.1 0.1 copy.12
  1.2 0.9 %copy.13 = bf16[3,32,3,32]{3,2,1,0:T(4,128)(2,1)S(1)} copy(bf16[3,32,3,32]{3,1,0,2:T(8,128)(2,1)} %bitcast.7) | data formatting | bytes 36864 | tf_op jit(solution)/shard_map/transpose | solution.py:379
  2.2 0.0 copy-start.4
  2.2 0.1 reshape.11.dec
  2.3 0.6 %copy-done.4 = bf16[128,32]{0,1:T(8,128)(2,1)S(1)} copy-done((bf16[128,32]{0,1:T(8,128)(2,1)S(1)}, bf16[128,32]{0,1:T(8,128)(2,1)}, u32[]{:S(2)}) %copy-start.4) | copy-done | bytes 8216
  2.9 0.0 copy-start.5
  2.9 0.0 copy-start.1
  2.9 0.0 copy-start.2
  2.9 0.1 copy.14.up
  3.0 0.6 %copy-done.5 = bf16[3,32]{1,0:T(4,128)(2,1)S(1)} copy-done((bf16[3,32]{1,0:T(4,128)(2,1)S(1)}, bf16[3,32]{1,0:T(4,128)(2,1)}, u32[]{:S(2)}) %copy-start.5) | copy-done | bytes 216
  3.6 0.0 copy-start.3
  3.6 0.0 copy-done
  3.6 0.1 copy-done.1
  3.6 0.0 copy-done.2
  3.6 0.6 %copy-done.3 = f32[32]{0:T(128)S(1)} copy-done((f32[32]{0:T(128)S(1)}, f32[32]{0:T(128)}, u32[]{:S(2)}) %copy-start.3) | copy-done | bytes 152
  4.2 45.1 %shard_map.82 = f32[3,2,128]{2,1,0:T(2,128)S(1)} custom-call(bf16[6,256,128]{2,1,0:T(8,128)(2,1)S(1)} %bitcast.5, bf16[224,64]{1,0:T(8,128)(2,1)S(1)} %pad.8.taps, bf16[128,32]{1,0:T(8,128)(2,1)S(1)} %copy.14.up, bf16[32,128]{1,0:T(8,128)(2,1)S(1)} %copy-done.2, bf16[3,32,32]{2,1,0:T(8,128)(2,1)S(1)} %copy-done.1, f32[32]{0:T(128)S(1)} %copy-done.3, ...), custom_call_target="tpu_custom_call" | custom-call | tf_op jit(solution)/shard_map/pallas_call | solution.py:385
  49.3 0.6 %copy.16 = f32[3,2,128]{2,1,0:T(2,128)} copy(f32[3,2,128]{2,1,0:T(2,128)S(1)} %shard_map.82) | data formatting | bytes 6144
  (2 shorter events, 0.0 us)
Async XLA Ops:
  0.0 3.6 %copy-start = (bf16[1,6,32,8,128]{4,3,2,1,0:T(8,128)(2,1)S(1)}, bf16[1,6,32,8,128]{4,3,2,1,0:T(8,128)(2,1)}, u32[]{:S(2)}) copy-start(bf16[1,6,32,8,128]{4,3,2,1,0:T(8,128)(2,1)} %param.8) | copy-start | bytes 1179652
  2.2 0.7 %copy-start.4 = (bf16[128,32]{0,1:T(8,128)(2,1)S(1)}, bf16[128,32]{0,1:T(8,128)(2,1)}, u32[]{:S(2)}) copy-start(bf16[128,32]{0,1:T(8,128)(2,1)} %param.10) | copy-start | bytes 24580
  2.9 0.7 %copy-start.5 = (bf16[3,32]{1,0:T(4,128)(2,1)S(1)}, bf16[3,32]{1,0:T(4,128)(2,1)}, u32[]{:S(2)}) copy-start(bf16[3,32]{1,0:T(4,128)(2,1)} %param.15) | copy-start | bytes 580
  2.9 0.8 %copy-start.1 = (bf16[3,32,32]{2,1,0:T(8,128)(2,1)S(1)}, bf16[3,32,32]{2,1,0:T(8,128)(2,1)}, u32[]{:S(2)}) copy-start(bf16[3,32,32]{2,1,0:T(8,128)(2,1)} %tap.1) | copy-start | bytes 18436
  2.9 0.8 %copy-start.2 = (bf16[32,128]{1,0:T(8,128)(2,1)S(1)}, bf16[32,128]{1,0:T(8,128)(2,1)}, u32[]{:S(2)}) copy-start(bf16[32,128]{1,0:T(8,128)(2,1)} %down.1) | copy-start | bytes 24580
  3.6 0.7 %copy-start.3 = (f32[32]{0:T(128)S(1)}, f32[32]{0:T(128)}, u32[]{:S(2)}) copy-start(f32[32]{0:T(128)} %opacity.1) | copy-start | bytes 388
where the time goes:
time: 50.2 us; the launch traced here: 49.9 us
  Pallas kernels  45.1 us (90%)
  local copies, waits for them, and re-layouts  4.77 us (10%)
    pallas_call x1, Pallas kernels, body(): pl.pallas_call(functools.partial(kernel, bands, slabs), out_shape=jax.Sha...  45.1 us
    unnamed x14, local copies, waits for them, and re-layouts  2.49 us
    reshape x2, local copies, waits for them, and re-layouts, body(): jnp.transpose(dw_weight, (3, 0, 1, 2)).reshape(224, 49)  1.2 us

commit v1 on v0

--- a/solution.py
+++ b/solution.py
@@ -10,6 +10,7 @@
 BF = jnp.bfloat16
 F32 = jnp.float32
 GROUPS = 4
+UNROLL = 8
 
 
 def iota(shape, dim):
@@ -24,11 +25,14 @@
     return 0.5 * x * (1.0 + jnp.tanh(0.7978845608028654 * (x + 0.044715 * (x * x * x))))
 
 
-def spread_rows(weight):
-    m, n = weight.shape
+def spread_rows(weight, turned=False):
+    m, n = weight.shape[::-1] if turned else weight.shape
     left = ((iota((8 * m, m), 0) >> 3) == iota((8 * m, m), 1)).astype(F32).astype(BF)
     right = (iota((n, 8 * n), 0) == (iota((n, 8 * n), 1) >> 3)).astype(F32).astype(BF)
-    full = dot(dot(left, weight).astype(BF), right)
+    first = lax.dot_general(
+        left, weight, (((1,), (1 if turned else 0,)), ((), ())), preferred_element_type=F32
+    )
+    full = dot(first.astype(BF), right)
     same = (iota(full.shape, 0) & 7) == (iota(full.shape, 1) & 7)
     return jnp.where(same, full, 0.0).astype(BF)
 
@@ -187,7 +191,7 @@
     send_rows(2)
 
     build_toeplitz()
-    ku[...] = spread_rows(up[...])
+    ku[...] = spread_rows(up[...], True)
     kd[...] = spread_rows(down[...])
     for k in range(3):
         kt[:, k * 256 : (k + 1) * 256] = spread_rows(tap[k])
@@ -229,15 +233,13 @@
 
         def conv(c, carry):
             cells = jnp.concatenate([xs[c], outer(xh[c], depth_rows)], 1)
-            part = dot(toep[c, :, 0:128], cells[0:128]) + dot(
-                toep[c, :, 128:depth_rows], cells[128:depth_rows]
-            )
+            part = dot(toep[c, :, 0:depth_rows], cells)
             total = shift_sum(part[:, 0:128], part[:, 128:256], 7, 48)
             for p in range(planes):
                 spread[p, pl.ds(pl.multiple_of(c * 8, 8), 8)] = total[p * 8 : (p + 1) * 8]
             return carry
 
-        lax.fori_loop(q * per, (q + 1) * per, conv, 0)
+        lax.fori_loop(q * per, (q + 1) * per, conv, 0, unroll=UNROLL)
 
     def mix(p):
         s = spread[p].reshape(32, 8, 128)
@@ -261,7 +263,7 @@
         mix(i * (planes - 1))
         return carry
 
-    lax.fori_loop(0, 2, edge, 0)
+    lax.fori_loop(0, 2, edge, 0, unroll=2)
     both(has["next"], mix_next.start)
     both(has["prev"], mix_prev.start)
 
@@ -269,7 +271,7 @@
         mix(p)
         return carry
 
-    lax.fori_loop(1, planes - 1, inner, 0)
+    lax.fori_loop(1, planes - 1, inner, 0, unroll=2)
     both(has["prev"], mix_next.wait_recv)
     both(has["next"], mix_prev.wait_recv)
 
@@ -342,7 +344,7 @@
         lines.append(jnp.concatenate([flat[y], outer(near[2, y], 32)], 1))
     lines.append(jnp.concatenate([near[1, 0], outer(near[4, 0], 32)], 1))
     for y in range(r):
-        part = dot(dec[...], jnp.concatenate(lines[y : y + 3], 0))
+        part = dot(dec[0], lines[y]) + dot(dec[1], lines[y + 1]) + dot(dec[2], lines[y + 2])
         decoded = gelu(shift_sum(part[:, 0:128], part[:, 128:256], 3, 32)).astype(BF)
         values = dot(outw[...], decoded)
         for o in range(3):
@@ -376,8 +378,7 @@
     r = 8 // slabs
     vol = volume.reshape(planes, 256, 128)
     taps = jnp.pad(jnp.transpose(dw_weight, (3, 0, 1, 2)).reshape(224, 49), ((0, 0), (0, 15)))
-    dec = jnp.transpose(decode_weight, (3, 0, 2, 1)).reshape(96, 96)
-    outw = jnp.pad(out_weight, ((0, 13), (0, 0)))
+    dec = jnp.transpose(decode_weight, (2, 3, 0, 1)).reshape(3, 96, 32)
     all_planes = planes + 6
     vmem = pl.BlockSpec(memory_space=pltpu.VMEM)
     smem = pl.BlockSpec(memory_space=pltpu.SMEM)
@@ -406,7 +407,7 @@
         compiler_params=pltpu.CompilerParams(
             collective_id=0, has_side_effects=True, vmem_limit_bytes=40 * 1024 * 1024
         ),
-    )(vol, taps, up_weight, down_weight, tap_weight, opacity_weight, dec, outw)
+    )(vol, taps, up_weight.T, down_weight, tap_weight, opacity_weight, dec, out_weight)
 
 
 def solution(mesh):

time: 50.2 us -> 41.3 us (0.82)
  Pallas kernels: 45.1 us -> 37.4 us
  local copies, waits for them, and re-layouts: 4.77 us -> 3.58 us
    pallas_call x1, Pallas kernels: 45.1 us -> 37.4 us  [body(): pl.pallas_call(functools.partial(kernel, bands, slabs), out_shape=jax.Sha...]
    transpose x1 -> x0, local copies, waits for them, and re-layouts: 0.94 us -> none  [body(): dec = jnp.transpose(decode_weight, (3, 0, 2, 1)).reshape(96, 96)]
    unnamed x14 -> x15, local copies, waits for them, and re-layouts: 2.49 us -> 2.41 us
where the time goes in v1:
time: 41.3 us; the launch traced here: 41 us
  Pallas kernels  37.4 us (91%)
  local copies, waits for them, and re-layouts  3.58 us (9%)
    pallas_call x1, Pallas kernels, body(): pl.pallas_call(functools.partial(kernel, bands, slabs), out_shape=jax.Sha...  37.4 us
    unnamed x15, local copies, waits for them, and re-layouts  2.41 us
    reshape x2, local copies, waits for them, and re-layouts, body(): jnp.transpose(dw_weight, (3, 0, 1, 2)).reshape(224, 49)  1.15 us

profile of v1, /device:TPU:0, one launch (start us, length us, event | category | flops | bytes accessed | tf_op | source)
XLA Modules:
  0.0 41.0 jit_solution(3952340489164790822)
XLA Ops:
  0.0 1.0 %reshape.10 = bf16[224,49]{0,1:T(8,128)(2,1)S(1)} reshape(bf16[7,32,7,7]{1,0,3,2:T(8,128)(2,1)} %bitcast.11) | data formatting | bytes 43904 | tf_op jit(solution)/shard_map/reshape | solution.py:380
  1.0 0.0 copy-start.5
  1.0 0.1 copy.10
  1.2 0.0 copy-start.1
  1.2 0.0 copy-start.2
  1.2 0.0 copy-start.3
  1.2 0.0 copy-start.4
  1.2 0.0 copy-start.6
  1.2 0.5 %copy-done.5 = bf16[3,32]{1,0:T(4,128)(2,1)S(1)} copy-done((bf16[3,32]{1,0:T(4,128)(2,1)S(1)}, bf16[3,32]{1,0:T(4,128)(2,1)}, u32[]{:S(2)}) %copy-start.5) | copy-done | bytes 216
  1.7 0.3 copy-done.1
  2.1 0.0 copy-done.2
  2.1 0.0 copy-done.3
  2.1 0.0 copy-done.4
  2.1 0.0 copy-done.6
  2.1 0.0 copy-start
  2.1 1.0 %copy-done = bf16[1,6,32,8,128]{4,3,2,1,0:T(8,128)(2,1)S(1)} copy-done((bf16[1,6,32,8,128]{4,3,2,1,0:T(8,128)(2,1)S(1)}, bf16[1,6,32,8,128]{4,3,2,1,0:T(8,128)(2,1)}, u32[]{:S(2)}) %copy-start) | copy-done | bytes 393240
  3.1 37.4 %shard_map.82 = f32[3,2,128]{2,1,0:T(2,128)S(1)} custom-call(bf16[6,256,128]{2,1,0:T(8,128)(2,1)S(1)} %bitcast.8, bf16[224,64]{1,0:T(8,128)(2,1)S(1)} %pad.4.taps, bf16[32,128]{1,0:T(8,128)(2,1)S(1)} %bitcast.10, bf16[32,128]{1,0:T(8,128)(2,1)S(1)} %copy-done.4, bf16[3,32,32]{2,1,0:T(8,128)(2,1)S(1)} %copy-done.2, f32[32]{0:T(128)S(1)} %copy-done.6, ...), custom_call_target="tpu_custom_call" | custom-call | tf_op jit(solution)/shard_map/pallas_call | solution.py:386
  40.5 0.6 %copy.12 = f32[3,2,128]{2,1,0:T(2,128)} copy(f32[3,2,128]{2,1,0:T(2,128)S(1)} %shard_map.82) | data formatting | bytes 6144
  (1 shorter events, 0.0 us)
Async XLA Ops:
  1.0 0.7 %copy-start.5 = (bf16[3,32]{1,0:T(4,128)(2,1)S(1)}, bf16[3,32]{1,0:T(4,128)(2,1)}, u32[]{:S(2)}) copy-start(bf16[3,32]{1,0:T(4,128)(2,1)} %outw.1) | copy-start | bytes 580
  1.2 0.9 %copy-start.1 = (bf16[32,32,3,3]{1,0,3,2:T(8,128)(2,1)S(1)}, bf16[32,32,3,3]{1,0,3,2:T(8,128)(2,1)}, u32[]{:S(2)}) copy-start(bf16[32,32,3,3]{1,0,3,2:T(8,128)(2,1)} %param.14) | copy-start | bytes 55300
  1.2 0.9 %copy-start.2 = (bf16[3,32,32]{2,1,0:T(8,128)(2,1)S(1)}, bf16[3,32,32]{2,1,0:T(8,128)(2,1)}, u32[]{:S(2)}) copy-start(bf16[3,32,32]{2,1,0:T(8,128)(2,1)} %tap.1) | copy-start | bytes 18436
  1.2 0.9 %copy-start.3 = (bf16[128,32]{0,1:T(8,128)(2,1)S(1)}, bf16[128,32]{0,1:T(8,128)(2,1)}, u32[]{:S(2)}) copy-start(bf16[128,32]{0,1:T(8,128)(2,1)} %param.10) | copy-start | bytes 24580
  1.2 0.9 %copy-start.4 = (bf16[32,128]{1,0:T(8,128)(2,1)S(1)}, bf16[32,128]{1,0:T(8,128)(2,1)}, u32[]{:S(2)}) copy-start(bf16[32,128]{1,0:T(8,128)(2,1)} %down.1) | copy-start | bytes 24580
  1.2 0.9 %copy-start.6 = (f32[32]{0:T(128)S(1)}, f32[32]{0:T(128)}, u32[]{:S(2)}) copy-start(f32[32]{0:T(128)} %opacity.1) | copy-start | bytes 388
  2.1 1.0 %copy-start = (bf16[1,6,32,8,128]{4,3,2,1,0:T(8,128)(2,1)S(1)}, bf16[1,6,32,8,128]{4,3,2,1,0:T(8,128)(2,1)}, u32[]{:S(2)}) copy-start(bf16[1,6,32,8,128]{4,3,2,1,0:T(8,128)(2,1)} %param.8) | copy-start | bytes 1179652

commit v2 on v1

--- a/solution.py
+++ b/solution.py
@@ -134,7 +134,7 @@
             dno[start + i] = high.reshape(128, 128).astype(BF)
             return carry
 
-        lax.fori_loop(0, n, one, 0)
+        lax.fori_loop(0, n, one, 0, unroll=3)
 
     def row_copies(k, start, n):
         return (
@@ -179,9 +179,14 @@
                 toep[c, k * 48 : (k + 1) * 48, 128:256] = jnp.concatenate(high, 0).astype(BF)
             return carry
 
-        lax.fori_loop(0, 32, one, 0)
+        lax.fori_loop(0, 32, one, 0, unroll=2)
 
     build_base()
+    build_toeplitz()
+    ku[...] = spread_rows(up[...], True)
+    kd[...] = spread_rows(down[...])
+    for k in range(3):
+        kt[:, k * 256 : (k + 1) * 256] = spread_rows(tap[k])
 
     both(has["prev"], to_next.wait_recv)
     pack_rows(front, 0, 3)
@@ -189,12 +194,6 @@
     both(has["next"], to_prev.wait_recv)
     pack_rows(back, 3 + planes, 3)
     send_rows(2)
-
-    build_toeplitz()
-    ku[...] = spread_rows(up[...], True)
-    kd[...] = spread_rows(down[...])
-    for k in range(3):
-        kt[:, k * 256 : (k + 1) * 256] = spread_rows(tap[k])
 
     for k in range(3):
         both(has["below"], rows[k][0].wait_recv)
@@ -272,14 +271,20 @@
         return carry
 
     lax.fori_loop(1, planes - 1, inner, 0, unroll=2)
+
+    def glow_of(p):
+        return dot(kt[...], mixed[p : p + 3].reshape(768, 128)).reshape(32, 8, 128)
+
+    glows = {p: glow_of(p) for p in range(1, planes - 1)}
     both(has["prev"], mix_next.wait_recv)
     both(has["next"], mix_prev.wait_recv)
+    glows[0], glows[planes - 1] = glow_of(0), glow_of(planes - 1)
 
     scale = 4.0 / (planes * slabs)
     light = jnp.ones((8, 128), F32)
     color[...] = jnp.zeros((256, 128), F32)
     for p in range(planes):
-        glow = dot(kt[...], mixed[p : p + 3].reshape(768, 128)).reshape(32, 8, 128)
+        glow = glows[p]
         logit = opacity[0] * glow[0]
         for c in range(1, 32):
             logit = logit + opacity[c] * glow[c]

time: 41.3 us -> 40.9 us (level)
  no operation moved by 1% of the time
where the time goes in v2:
time: 40.9 us; the launch traced here: 40.6 us
  Pallas kernels  37 us (90%)
  local copies, waits for them, and re-layouts  3.58 us (9%)
    pallas_call x1, Pallas kernels, body(): pl.pallas_call(functools.partial(kernel, bands, slabs), out_shape=jax.Sha...  37 us
    unnamed x15, local copies, waits for them, and re-layouts  2.41 us
    reshape x2, local copies, waits for them, and re-layouts, body(): jnp.transpose(dw_weight, (3, 0, 1, 2)).reshape(224, 49)  1.15 us

profile of v2, /device:TPU:0, one launch (start us, length us, event | category | flops | bytes accessed | tf_op | source)
XLA Modules:
  0.0 40.6 jit_solution(16671322008807328745)
XLA Ops:
  0.0 1.0 %reshape.10 = bf16[224,49]{0,1:T(8,128)(2,1)S(1)} reshape(bf16[7,32,7,7]{1,0,3,2:T(8,128)(2,1)} %bitcast.11) | data formatting | bytes 43904 | tf_op jit(solution)/shard_map/reshape | solution.py:385
  1.0 0.0 copy-start.5
  1.0 0.1 copy.10
  1.2 0.0 copy-start.1
  1.2 0.0 copy-start.2
  1.2 0.0 copy-start.3
  1.2 0.0 copy-start.4
  1.2 0.0 copy-start.6
  1.2 0.5 %copy-done.5 = bf16[3,32]{1,0:T(4,128)(2,1)S(1)} copy-done((bf16[3,32]{1,0:T(4,128)(2,1)S(1)}, bf16[3,32]{1,0:T(4,128)(2,1)}, u32[]{:S(2)}) %copy-start.5) | copy-done | bytes 216
  1.7 0.3 copy-done.1
  2.1 0.0 copy-done.2
  2.1 0.0 copy-done.3
  2.1 0.0 copy-done.4
  2.1 0.0 copy-done.6
  2.1 0.0 copy-start
  2.1 1.0 %copy-done = bf16[1,6,32,8,128]{4,3,2,1,0:T(8,128)(2,1)S(1)} copy-done((bf16[1,6,32,8,128]{4,3,2,1,0:T(8,128)(2,1)S(1)}, bf16[1,6,32,8,128]{4,3,2,1,0:T(8,128)(2,1)}, u32[]{:S(2)}) %copy-start) | copy-done | bytes 393240
  3.1 37.0 %shard_map.82 = f32[3,2,128]{2,1,0:T(2,128)S(1)} custom-call(bf16[6,256,128]{2,1,0:T(8,128)(2,1)S(1)} %bitcast.8, bf16[224,64]{1,0:T(8,128)(2,1)S(1)} %pad.4.taps, bf16[32,128]{1,0:T(8,128)(2,1)S(1)} %bitcast.10, bf16[32,128]{1,0:T(8,128)(2,1)S(1)} %copy-done.4, bf16[3,32,32]{2,1,0:T(8,128)(2,1)S(1)} %copy-done.2, f32[32]{0:T(128)S(1)} %copy-done.6, ...), custom_call_target="tpu_custom_call" | custom-call | tf_op jit(solution)/shard_map/pallas_call | solution.py:391
  40.1 0.6 %copy.12 = f32[3,2,128]{2,1,0:T(2,128)} copy(f32[3,2,128]{2,1,0:T(2,128)S(1)} %shard_map.82) | data formatting | bytes 6144
  (1 shorter events, 0.0 us)
Async XLA Ops:
  1.0 0.7 %copy-start.5 = (bf16[3,32]{1,0:T(4,128)(2,1)S(1)}, bf16[3,32]{1,0:T(4,128)(2,1)}, u32[]{:S(2)}) copy-start(bf16[3,32]{1,0:T(4,128)(2,1)} %outw.1) | copy-start | bytes 580
  1.2 0.9 %copy-start.1 = (bf16[32,32,3,3]{1,0,3,2:T(8,128)(2,1)S(1)}, bf16[32,32,3,3]{1,0,3,2:T(8,128)(2,1)}, u32[]{:S(2)}) copy-start(bf16[32,32,3,3]{1,0,3,2:T(8,128)(2,1)} %param.14) | copy-start | bytes 55300
  1.2 0.9 %copy-start.2 = (bf16[3,32,32]{2,1,0:T(8,128)(2,1)S(1)}, bf16[3,32,32]{2,1,0:T(8,128)(2,1)}, u32[]{:S(2)}) copy-start(bf16[3,32,32]{2,1,0:T(8,128)(2,1)} %tap.1) | copy-start | bytes 18436
  1.2 0.9 %copy-start.3 = (bf16[128,32]{0,1:T(8,128)(2,1)S(1)}, bf16[128,32]{0,1:T(8,128)(2,1)}, u32[]{:S(2)}) copy-start(bf16[128,32]{0,1:T(8,128)(2,1)} %param.10) | copy-start | bytes 24580
  1.2 0.9 %copy-start.4 = (bf16[32,128]{1,0:T(8,128)(2,1)S(1)}, bf16[32,128]{1,0:T(8,128)(2,1)}, u32[]{:S(2)}) copy-start(bf16[32,128]{1,0:T(8,128)(2,1)} %down.1) | copy-start | bytes 24580
  1.2 0.9 %copy-start.6 = (f32[32]{0:T(128)S(1)}, f32[32]{0:T(128)}, u32[]{:S(2)}) copy-start(f32[32]{0:T(128)} %opacity.1) | copy-start | bytes 388
  2.1 1.0 %copy-start = (bf16[1,6,32,8,128]{4,3,2,1,0:T(8,128)(2,1)S(1)}, bf16[1,6,32,8,128]{4,3,2,1,0:T(8,128)(2,1)}, u32[]{:S(2)}) copy-start(bf16[1,6,32,8,128]{4,3,2,1,0:T(8,128)(2,1)} %param.8) | copy-start | bytes 1179652
